TPU v7x, 32 devices: a whole 2x2x4 slice. The times are simulated.
32 devices in a mesh: groups: 2 (over y), gx: 8 (over z, x), gy: 2 (over core).
Axes of the slice: x: 2, y: 2, z: 4, core: 2. Of those that a mesh axis runs over, the one named last changes fastest.
Arguments:
- adj_tracer: float32 [20, 256, 512], P('groups', 'gx', 'gy'), parts along dimension 0, may hold values from -6 to 6
- adj_east: float32 [20, 256, 512], P('groups', 'gx', 'gy'), parts along dimension 0, may hold values from -6 to 6
- adj_north: float32 [20, 256, 512], P('groups', 'gx', 'gy'), parts along dimension 0, may hold values from -6 to 6
- flow_east: float32 [20, 256, 512], P('groups', 'gx', 'gy'), parts along dimension 0, may hold values from -0.6 to 0.6
- flow_north: float32 [20, 256, 512], P('groups', 'gx', 'gy'), parts along dimension 0, may hold values from -0.6 to 0.6
- mixing: float32 [20, 256, 512], P('groups', 'gx', 'gy'), parts along dimension 0, may hold values from 0.02 to 0.2
- buoyancy: float32 [10], replicated, may hold values from 0.2 to 0.8
- coriolis: float32 [512], P('gy'), may hold values from -0.5 to 0.5
- column_depth: int32 [512, 512], P(('groups', 'gx'), 'gy'), parts along dimension 0, may hold values from 0 to 10
- adj_surface: float32 [512, 512], P(('groups', 'gx'), 'gy'), parts along dimension 0, may hold values from -40 to 40
- surface_diag: float32 [512, 512], P(('groups', 'gx'), 'gy'), parts along dimension 0, may hold values from 0.05 to 0.5
- prior_surface: float32 [512, 512], P(('groups', 'gx'), 'gy'), parts along dimension 0, may hold values from -6 to 6
Outputs:
- tracer_out: float32 [20, 256, 512], P('groups', 'gx', 'gy'), parts along dimension 0
- east_out: float32 [20, 256, 512], P('groups', 'gx', 'gy'), parts along dimension 0
- north_out: float32 [20, 256, 512], P('groups', 'gx', 'gy'), parts along dimension 0
- surface_solution: float32 [512, 512], P(('groups', 'gx'), 'gy'), parts along dimension 0
There are 2 independent parts, one for each index of `groups`. A program takes and returns all parts, laid end to end along the dimension named above; an argument that names none is the same for every part. Nothing has to cross between parts.
Inputs may be any that keep to these rules, and one draw needn't show every extreme that they name: `column_depth`: 0 marks a land column.
All inputs are finite; a program needn't handle non-finite values.
Results may differ from a plain program's by a relative error of at most 0.0001.
Values sent between devices are 32-bit elements; how exact they have to be, the bound alone decides.
A program may use at most 64 MiB of HBM per device.

v0:
```python
import jax
import jax.numpy as jnp
from jax import lax
from jax.sharding import PartitionSpec as P

SUB = 3
ITERS = 3


STIFFNESS = 0.1


def extended(cells, sides, width):
    for axis, dim in sides:
        count = lax.axis_size(axis)
        head = lax.slice_in_dim(cells, 0, width, axis=dim)
        tail = lax.slice_in_dim(cells, cells.shape[dim] - width, cells.shape[dim], axis=dim)
        cells = jnp.concatenate(
            [
                lax.ppermute(tail, axis, [(i, (i + 1) % count) for i in range(count)]),
                cells,
                lax.ppermute(head, axis, [((i + 1) % count, i) for i in range(count)]),
            ],
            axis=dim,
        )
    return cells


def shifted(padded):
    return (
        padded[..., 1:-1, 1:-1],
        padded[..., 2:, 1:-1],
        padded[..., :-2, 1:-1],
        padded[..., 1:-1, 2:],
        padded[..., 1:-1, :-2],
    )


def advance(moving, statics, levels, buoyancy, heights):
    courant_east = statics[:levels, 1:-1, 1:-1]
    courant_north = statics[levels : 2 * levels, 1:-1, 1:-1]
    mix_here, mix_east, mix_west, mix_north, mix_south = shifted(statics[2 * levels : 3 * levels])
    rotation = statics[3 * levels, 1:-1, 1:-1]
    wet_mask = (heights < statics[3 * levels + 1][None]).astype(jnp.float32)
    wet_here, wet_east, wet_west, wet_north, wet_south = shifted(wet_mask)
    face_east = 0.5 * (mix_here + mix_east) * wet_here * wet_east
    face_west = 0.5 * (mix_west + mix_here) * wet_west * wet_here
    face_north = 0.5 * (mix_here + mix_north) * wet_here * wet_north
    face_south = 0.5 * (mix_south + mix_here) * wet_south * wet_here
    centre, east_side, west_side, north_side, south_side = shifted(moving)
    carried = (
        centre
        + courant_east * (east_side - west_side) * 0.5
        + courant_north * (north_side - south_side) * 0.5
        + face_east * (east_side - centre)
        + face_west * (west_side - centre)
        + face_north * (north_side - centre)
        + face_south * (south_side - centre)
    )
    lifted = buoyancy[:, None, None] * (
        wet_here * wet_east * centre[1]
        - wet_west * wet_here * west_side[1]
        + wet_here * wet_north * centre[2]
        - wet_south * wet_here * south_side[2]
    )
    tracer = wet_here * (carried[0] + lifted)
    east_new = wet_here * (carried[1] - rotation * centre[2])
    north_new = wet_here * (carried[2] + rotation * centre[1])
    return jnp.stack([tracer, east_new, north_new])


def plane_halo(stacked):
    return extended(stacked, (("gx", 1), ("gy", 2)), 1)


def total_norm(field):
    return lax.psum(jnp.sum(field * field), ("gx", "gy"))


def per_device(
    adj_tracer,
    adj_east,
    adj_north,
    flow_east,
    flow_north,
    mixing,
    buoyancy,
    coriolis,
    column_depth,
    adj_surface,
    surface_diag,
    prior_surface,
):
    levels, tile_cols, tile_rows = adj_tracer.shape
    row_index = lax.axis_index("gy") * tile_rows + jnp.arange(tile_rows)
    total_rows = lax.axis_size("gy") * tile_rows
    interior = ((row_index > 0) & (row_index < total_rows - 1)).astype(jnp.float32)
    depth_eff = column_depth.astype(jnp.float32) * interior[None, :]
    heights = jnp.arange(levels, dtype=jnp.float32)[:, None, None]
    wet_local = (heights < depth_eff[None]).astype(jnp.float32)
    rotation = jnp.broadcast_to(coriolis[None, :], (tile_cols, tile_rows))
    statics = jnp.concatenate(
        [flow_east, flow_north, mixing, rotation[None], depth_eff[None]], axis=0
    )
    fields = wet_local[None] * jnp.stack([adj_tracer, adj_east, adj_north])
    static_ext = extended(statics, (("gx", 1), ("gy", 2)), 1)
    moving = fields
    first_sub = 0
    for substep in range(first_sub, SUB):
        padded = extended(
            moving.reshape(3 * levels, tile_cols, tile_rows), (("gx", 1), ("gy", 2)), 1
        )
        moving = advance(
            padded.reshape(3, levels, tile_cols + 2, tile_rows + 2),
            static_ext,
            levels,
            buoyancy,
            heights,
        )
    wet_edge = (heights < static_ext[3 * levels + 1][None]).astype(jnp.float32)
    edge_here, edge_east, edge_west, edge_north, edge_south = shifted(wet_edge)
    reach_east = STIFFNESS * jnp.sum(edge_here * edge_east, axis=0)
    reach_west = STIFFNESS * jnp.sum(edge_west * edge_here, axis=0)
    reach_north = STIFFNESS * jnp.sum(edge_here * edge_north, axis=0)
    reach_south = STIFFNESS * jnp.sum(edge_south * edge_here, axis=0)

    def surface_operator(padded):
        centre, east_side, west_side, north_side, south_side = shifted(padded)
        return (
            surface_diag * centre
            + reach_east * (centre - east_side)
            + reach_west * (centre - west_side)
            + reach_north * (centre - north_side)
            + reach_south * (centre - south_side)
        )

    column_east = jnp.sum(moving[1], axis=0)
    column_north = jnp.sum(moving[2], axis=0)
    wet_column = (depth_eff > 0).astype(jnp.float32)
    solution = wet_column * prior_surface
    planes = plane_halo(jnp.stack([column_east, column_north, solution]))
    right_side = wet_column * (
        adj_surface
        + 0.5 * (planes[0, :-2, 1:-1] - planes[0, 2:, 1:-1])
        + 0.5 * (planes[1, 1:-1, :-2] - planes[1, 1:-1, 2:])
    )
    residual = right_side - surface_operator(planes[2])
    solution_pad = planes[2]
    direction = residual
    norm_now = total_norm(residual)
    for iteration in range(ITERS):
        direction_pad = plane_halo(direction[None])[0]
        mapped = surface_operator(direction_pad)
        step_size = norm_now / lax.psum(jnp.sum(direction * mapped), ("gx", "gy"))
        solution = solution + step_size * direction
        solution_pad = solution_pad + step_size * direction_pad
        if iteration + 1 < ITERS:
            residual = residual - step_size * mapped
            norm_next = total_norm(residual)
            direction = residual + norm_next / norm_now * direction
            norm_now = norm_next
    final = plane_halo(solution[None])[0]
    grad_east = 0.5 * (final[2:, 1:-1] - final[:-2, 1:-1])
    grad_north = 0.5 * (final[1:-1, 2:] - final[1:-1, :-2])
    east_out = moving[1] + wet_local * grad_east[None]
    north_out = moving[2] + wet_local * grad_north[None]
    return (moving[0], east_out, north_out, solution)


def solution(mesh):
    placed = (
        P("groups", "gx", "gy"),
        P("groups", "gx", "gy"),
        P("groups", "gx", "gy"),
        P("groups", "gx", "gy"),
        P("groups", "gx", "gy"),
        P("groups", "gx", "gy"),
        P(),
        P("gy"),
        P(("groups", "gx"), "gy"),
        P(("groups", "gx"), "gy"),
        P(("groups", "gx"), "gy"),
        P(("groups", "gx"), "gy"),
    )
    return jax.shard_map(
        per_device,
        mesh=mesh,
        in_specs=placed,
        out_specs=(
            P("groups", "gx", "gy"),
            P("groups", "gx", "gy"),
            P("groups", "gx", "gy"),
            P(("groups", "gx"), "gy"),
        ),
        check_vma=False,
    )
```

profile of v0, /device:TPU:0, one launch (start us, length us, event | category | flops | bytes accessed | tf_op | source)
XLA Modules:
  0.0 288.4 jit_solution(9090359916345949382)
XLA Ops:
  3.6 3.0 %collective-permute-start.4 = (f32[30,1,256]{2,1,0:T(1,128)S(1)}, f32[30,1,256]{2,1,0:T(1,128)S(1)}, u32[]{:S(2)}, u32[]{:S(2)}) collective-permute-start(f32[30,1,256]{2,1,0:T(1,128)S(1)} %get-tuple-element.54), channel_id=1, source_target_pairs={{0,2},{2,4},{4,6},{6,8},{8,10},{10,12},{12,14},{14,0},{1,3},{3,5},... | collective-permute-start | bytes 92168 | tf_op jit(solution)/shard_map/ppermute | solution.py:20
  6.6 3.1 %collective-permute-start.5 = (f32[30,1,256]{2,1,0:T(1,128)S(1)}, f32[30,1,256]{2,1,0:T(1,128)S(1)}, u32[]{:S(2)}, u32[]{:S(2)}) collective-permute-start(f32[30,1,256]{2,1,0:T(1,128)S(1)} %get-tuple-element.55), channel_id=1, source_target_pairs={{2,0},{4,2},{6,4},{8,6},{10,8},{12,10},{14,12},{0,14},{3,1},{5,3},... | collective-permute-start | bytes 92168 | tf_op jit(solution)/shard_map/ppermute | solution.py:22
  9.9 4.7 %collective-permute-start.1 = (f32[32,1,256]{2,1,0:T(1,128)S(1)}, f32[32,1,256]{2,1,0:T(1,128)S(1)}, u32[]{:S(2)}, u32[]{:S(2)}) collective-permute-start(f32[32,1,256]{2,1,0:T(1,128)S(1)} %get-tuple-element.49), channel_id=1, source_target_pairs={{2,0},{4,2},{6,4},{8,6},{10,8},{12,10},{14,12},{0,14},{3,1},{5,3},... | collective-permute-start | bytes 98312 | tf_op jit(solution)/shard_map/ppermute | solution.py:22
  22.3 2.4 pad_maximum_fusion
  24.7 1.9 copy.41
  26.6 1.9 copy.40
  29.9 1.7 fusion.50
  31.6 2.0 fusion.60
  35.7 4.7 %collective-permute-start.9 = (f32[30,1,256]{2,1,0:T(1,128)S(1)}, f32[30,1,256]{2,1,0:T(1,128)S(1)}, u32[]{:S(2)}, u32[]{:S(2)}) collective-permute-start(f32[30,1,256]{2,1,0:T(1,128)S(1)} %get-tuple-element.53), channel_id=1, source_target_pairs={{2,0},{4,2},{6,4},{8,6},{10,8},{12,10},{14,12},{0,14},{3,1},{5,3},... | collective-permute-start | bytes 92168 | tf_op jit(solution)/shard_map/ppermute | solution.py:22
  40.5 1.9 collective-permute-done.8
  49.4 2.4 pad_maximum_fusion.1
  54.0 5.0 %collective-permute-start.13 = (f32[30,1,256]{2,1,0:T(1,128)S(1)}, f32[30,1,256]{2,1,0:T(1,128)S(1)}, u32[]{:S(2)}, u32[]{:S(2)}) collective-permute-start(f32[30,1,256]{2,1,0:T(1,128)S(1)} %get-tuple-element.51), channel_id=1, source_target_pairs={{2,0},{4,2},{6,4},{8,6},{10,8},{12,10},{14,12},{0,14},{3,1},{5,3},... | collective-permute-start | bytes 92168 | tf_op jit(solution)/shard_map/ppermute | solution.py:22
  58.9 1.6 collective-permute-done.12
  67.6 2.3 pad_maximum_fusion.2
  72.7 5.0 %collective-permute-start.17 = (f32[3,1,256]{2,1,0:T(1,128)S(1)}, f32[3,1,256]{2,1,0:T(1,128)S(1)}, u32[]{:S(2)}, u32[]{:S(2)}) collective-permute-start(f32[3,1,256]{2,1,0:T(1,128)S(1)} %get-tuple-element.60), channel_id=1, source_target_pairs={{2,0},{4,2},{6,4},{8,6},{10,8},{12,10},{14,12},{0,14},{3,1},{5,3},... | collective-permute-start | bytes 9224 | tf_op jit(solution)/shard_map/ppermute | solution.py:22
  81.2 4.8 %collective-permute-start.21 = (f32[1,1,256]{2,1,0:T(1,128)S(1)}, f32[1,1,256]{2,1,0:T(1,128)S(1)}, u32[]{:S(2)}, u32[]{:S(2)}) collective-permute-start(f32[1,1,256]{2,1,0:T(1,128)S(1)} %get-tuple-element.80), channel_id=1, source_target_pairs={{2,0},{4,2},{6,4},{8,6},{10,8},{12,10},{14,12},{0,14},{3,1},{5,3},... | collective-permute-start | bytes 3080 | tf_op jit(solution)/shard_map/ppermute | solution.py:22
  89.8 34.8 %all-reduce = (f32[]{:T(128)}, f32[]{:T(128)}) all-reduce(f32[]{:T(128)} %get-tuple-element.13, f32[]{:T(128)} %get-tuple-element.12), channel_id=1, replica_groups=mesh['groups'=2,'gx'=8,'gy'=2] {'gx','gy'}, use_global_device_ids=true, to_apply=%region_7.0 | all-reduce | flops 2 | bytes 16 | tf_op jit(solution)/shard_map/psum | solution.py:77
  126.6 30.1 %psum.44 = f32[]{:T(128)} all-reduce(f32[]{:T(128)} %get-tuple-element.18), channel_id=1, replica_groups=mesh['groups'=2,'gx'=8,'gy'=2] {'gx','gy'}, use_global_device_ids=true, to_apply=%region_11.0 | all-reduce | flops 1 | bytes 8 | tf_op jit(solution)/shard_map/psum | solution.py:77
  158.1 4.7 %collective-permute-start.25 = (f32[1,1,256]{2,1,0:T(1,128)S(1)}, f32[1,1,256]{2,1,0:T(1,128)S(1)}, u32[]{:S(2)}, u32[]{:S(2)}) collective-permute-start(f32[1,1,256]{2,1,0:T(1,128)S(1)} %get-tuple-element.78), channel_id=1, source_target_pairs={{2,0},{4,2},{6,4},{8,6},{10,8},{12,10},{14,12},{0,14},{3,1},{5,3},... | collective-permute-start | bytes 3080 | tf_op jit(solution)/shard_map/ppermute | solution.py:22
  166.6 34.8 %psum.45 = f32[]{:T(128)} all-reduce(f32[]{:T(128)} %get-tuple-element.16), channel_id=1, replica_groups=mesh['groups'=2,'gx'=8,'gy'=2] {'gx','gy'}, use_global_device_ids=true, to_apply=%region_13.0 | all-reduce | flops 1 | bytes 8 | tf_op jit(solution)/shard_map/psum | solution.py:154
  203.3 30.1 %psum.46 = f32[]{:T(128)} all-reduce(f32[]{:T(128)} %multiply_reduce_fusion), channel_id=1, replica_groups=mesh['groups'=2,'gx'=8,'gy'=2] {'gx','gy'}, use_global_device_ids=true, to_apply=%region_15.0 | all-reduce | flops 1 | bytes 8 | tf_op jit(solution)/shard_map/psum | solution.py:77
  234.9 4.7 %collective-permute-start.29 = (f32[1,1,256]{2,1,0:T(1,128)S(1)}, f32[1,1,256]{2,1,0:T(1,128)S(1)}, u32[]{:S(2)}, u32[]{:S(2)}) collective-permute-start(f32[1,1,256]{2,1,0:T(1,128)S(1)} %get-tuple-element.76), channel_id=1, source_target_pairs={{2,0},{4,2},{6,4},{8,6},{10,8},{12,10},{14,12},{0,14},{3,1},{5,3},... | collective-permute-start | bytes 3080 | tf_op jit(solution)/shard_map/ppermute | solution.py:22
  243.4 34.8 %psum.47 = f32[]{:T(128)} all-reduce(f32[]{:T(128)} %fusion.71), channel_id=1, replica_groups=mesh['groups'=2,'gx'=8,'gy'=2] {'gx','gy'}, use_global_device_ids=true, to_apply=%region_17.0 | all-reduce | flops 1 | bytes 8 | tf_op jit(solution)/shard_map/psum | solution.py:154
  279.6 4.7 %collective-permute-start.33 = (f32[1,1,256]{2,1,0:T(1,128)S(1)}, f32[1,1,256]{2,1,0:T(1,128)S(1)}, u32[]{:S(2)}, u32[]{:S(2)}) collective-permute-start(f32[1,1,256]{2,1,0:T(1,128)S(1)} %get-tuple-element.74), channel_id=1, source_target_pairs={{2,0},{4,2},{6,4},{8,6},{10,8},{12,10},{14,12},{0,14},{3,1},{5,3},... | collective-permute-start | bytes 3080 | tf_op jit(solution)/shard_map/ppermute | solution.py:22
  (208 shorter events, 53.3 us)
Async XLA Ops:
  3.6 11.1 %collective-permute-start.4 = (f32[30,1,256]{2,1,0:T(1,128)S(1)}, f32[30,1,256]{2,1,0:T(1,128)S(1)}, u32[]{:S(2)}, u32[]{:S(2)}) collective-permute-start(f32[30,1,256]{2,1,0:T(1,128)S(1)} %get-tuple-element.54), channel_id=1, source_target_pairs={{0,2},{2,4},{4,6},{6,8},{8,10},{10,12},{12,14},{14,0},{1,3},{3,5},... | collective-permute-start | bytes 92168 | tf_op jit(solution)/shard_map/ppermute | solution.py:20
  6.6 8.1 %collective-permute-start.5 = (f32[30,1,256]{2,1,0:T(1,128)S(1)}, f32[30,1,256]{2,1,0:T(1,128)S(1)}, u32[]{:S(2)}, u32[]{:S(2)}) collective-permute-start(f32[30,1,256]{2,1,0:T(1,128)S(1)} %get-tuple-element.55), channel_id=1, source_target_pairs={{2,0},{4,2},{6,4},{8,6},{10,8},{12,10},{14,12},{0,14},{3,1},{5,3},... | collective-permute-start | bytes 92168 | tf_op jit(solution)/shard_map/ppermute | solution.py:22
  9.9 7.6 %collective-permute-start = (f32[32,1,256]{2,1,0:T(1,128)S(1)}, f32[32,1,256]{2,1,0:T(1,128)S(1)}, u32[]{:S(2)}, u32[]{:S(2)}) collective-permute-start(f32[32,1,256]{2,1,0:T(1,128)S(1)} %get-tuple-element.48), channel_id=1, source_target_pairs={{0,2},{2,4},{4,6},{6,8},{8,10},{10,12},{12,14},{14,0},{1,3},{3,5},... | collective-permute-start | bytes 98312 | tf_op jit(solution)/shard_map/ppermute | solution.py:20
  9.9 7.5 %collective-permute-start.1 = (f32[32,1,256]{2,1,0:T(1,128)S(1)}, f32[32,1,256]{2,1,0:T(1,128)S(1)}, u32[]{:S(2)}, u32[]{:S(2)}) collective-permute-start(f32[32,1,256]{2,1,0:T(1,128)S(1)} %get-tuple-element.49), channel_id=1, source_target_pairs={{2,0},{4,2},{6,4},{8,6},{10,8},{12,10},{14,12},{0,14},{3,1},{5,3},... | collective-permute-start | bytes 98312 | tf_op jit(solution)/shard_map/ppermute | solution.py:22
  16.9 4.3 %collective-permute-start.7 = (f32[30,34,1]{1,2,0:T(1,128)S(1)}, f32[30,34,1]{1,2,0:T(1,128)S(1)}, u32[]{:S(2)}, u32[]{:S(2)}) collective-permute-start(f32[30,34,1]{1,2,0:T(1,128)S(1)} %copy.43), channel_id=1, source_target_pairs={{1,0},{0,1},{3,2},{2,3},{5,4},{4,5},{7,6},{6,7},{9,8},{8,9},{11,10... | collective-permute-start | bytes 12248 | tf_op jit(solution)/shard_map/ppermute | solution.py:22
  17.0 3.9 %collective-permute-start.6 = (f32[30,34,1]{1,2,0:T(1,128)S(1)}, f32[30,34,1]{1,2,0:T(1,128)S(1)}, u32[]{:S(2)}, u32[]{:S(2)}) collective-permute-start(f32[30,34,1]{1,2,0:T(1,128)S(1)} %copy.42), channel_id=1, source_target_pairs={{0,1},{1,0},{2,3},{3,2},{4,5},{5,4},{6,7},{7,6},{8,9},{9,8},{10,11... | collective-permute-start | bytes 12248 | tf_op jit(solution)/shard_map/ppermute | solution.py:20
  20.3 6.3 %collective-permute-start.2 = (f32[32,34,1]{1,0,2:T(8,128)}, f32[32,34,1]{1,0,2:T(8,128)}, u32[]{:S(2)}, u32[]{:S(2)}) collective-permute-start(f32[32,34,1]{1,0,2:T(8,128)} %copy.38), channel_id=1, source_target_pairs={{0,1},{1,0},{2,3},{3,2},{4,5},{5,4},{6,7},{7,6},{8,9},{9,8},{10,11... | collective-permute-start | bytes 13064 | tf_op jit(solution)/shard_map/ppermute | solution.py:20
  20.4 4.3 %collective-permute-start.3 = (f32[32,34,1]{1,0,2:T(8,128)}, f32[32,34,1]{1,0,2:T(8,128)}, u32[]{:S(2)}, u32[]{:S(2)}) collective-permute-start(f32[32,34,1]{1,0,2:T(8,128)} %copy.39), channel_id=1, source_target_pairs={{1,0},{0,1},{3,2},{2,3},{5,4},{4,5},{7,6},{6,7},{9,8},{8,9},{11,10... | collective-permute-start | bytes 13064 | tf_op jit(solution)/shard_map/ppermute | solution.py:22
  35.7 6.6 %collective-permute-start.8 = (f32[30,1,256]{2,1,0:T(1,128)S(1)}, f32[30,1,256]{2,1,0:T(1,128)S(1)}, u32[]{:S(2)}, u32[]{:S(2)}) collective-permute-start(f32[30,1,256]{2,1,0:T(1,128)S(1)} %get-tuple-element.52), channel_id=1, source_target_pairs={{0,2},{2,4},{4,6},{6,8},{8,10},{10,12},{12,14},{14,0},{1,3},{3,5},... | collective-permute-start | bytes 92168 | tf_op jit(solution)/shard_map/ppermute | solution.py:20
  35.7 6.6 %collective-permute-start.9 = (f32[30,1,256]{2,1,0:T(1,128)S(1)}, f32[30,1,256]{2,1,0:T(1,128)S(1)}, u32[]{:S(2)}, u32[]{:S(2)}) collective-permute-start(f32[30,1,256]{2,1,0:T(1,128)S(1)} %get-tuple-element.53), channel_id=1, source_target_pairs={{2,0},{4,2},{6,4},{8,6},{10,8},{12,10},{14,12},{0,14},{3,1},{5,3},... | collective-permute-start | bytes 92168 | tf_op jit(solution)/shard_map/ppermute | solution.py:22
  45.1 2.0 collective-permute-start.10
  53.9 6.6 %collective-permute-start.12 = (f32[30,1,256]{2,1,0:T(1,128)S(1)}, f32[30,1,256]{2,1,0:T(1,128)S(1)}, u32[]{:S(2)}, u32[]{:S(2)}) collective-permute-start(f32[30,1,256]{2,1,0:T(1,128)S(1)} %get-tuple-element.50), channel_id=1, source_target_pairs={{0,2},{2,4},{4,6},{6,8},{8,10},{10,12},{12,14},{14,0},{1,3},{3,5},... | collective-permute-start | bytes 92168 | tf_op jit(solution)/shard_map/ppermute | solution.py:20
  54.0 6.6 %collective-permute-start.13 = (f32[30,1,256]{2,1,0:T(1,128)S(1)}, f32[30,1,256]{2,1,0:T(1,128)S(1)}, u32[]{:S(2)}, u32[]{:S(2)}) collective-permute-start(f32[30,1,256]{2,1,0:T(1,128)S(1)} %get-tuple-element.51), channel_id=1, source_target_pairs={{2,0},{4,2},{6,4},{8,6},{10,8},{12,10},{14,12},{0,14},{3,1},{5,3},... | collective-permute-start | bytes 92168 | tf_op jit(solution)/shard_map/ppermute | solution.py:22
  63.3 2.0 collective-permute-start.14
  72.7 6.6 %collective-permute-start.16 = (f32[3,1,256]{2,1,0:T(1,128)S(1)}, f32[3,1,256]{2,1,0:T(1,128)S(1)}, u32[]{:S(2)}, u32[]{:S(2)}) collective-permute-start(f32[3,1,256]{2,1,0:T(1,128)S(1)} %get-tuple-element.59), channel_id=1, source_target_pairs={{0,2},{2,4},{4,6},{6,8},{8,10},{10,12},{12,14},{14,0},{1,3},{3,5},... | collective-permute-start | bytes 9224 | tf_op jit(solution)/shard_map/ppermute | solution.py:20
  72.7 6.5 %collective-permute-start.17 = (f32[3,1,256]{2,1,0:T(1,128)S(1)}, f32[3,1,256]{2,1,0:T(1,128)S(1)}, u32[]{:S(2)}, u32[]{:S(2)}) collective-permute-start(f32[3,1,256]{2,1,0:T(1,128)S(1)} %get-tuple-element.60), channel_id=1, source_target_pairs={{2,0},{4,2},{6,4},{8,6},{10,8},{12,10},{14,12},{0,14},{3,1},{5,3},... | collective-permute-start | bytes 9224 | tf_op jit(solution)/shard_map/ppermute | solution.py:22
  81.1 6.4 %collective-permute-start.20 = (f32[1,1,256]{2,1,0:T(1,128)S(1)}, f32[1,1,256]{2,1,0:T(1,128)S(1)}, u32[]{:S(2)}, u32[]{:S(2)}) collective-permute-start(f32[1,1,256]{2,1,0:T(1,128)S(1)} %get-tuple-element.79), channel_id=1, source_target_pairs={{0,2},{2,4},{4,6},{6,8},{8,10},{10,12},{12,14},{14,0},{1,3},{3,5},... | collective-permute-start | bytes 3080 | tf_op jit(solution)/shard_map/ppermute | solution.py:20
  81.2 6.3 %collective-permute-start.21 = (f32[1,1,256]{2,1,0:T(1,128)S(1)}, f32[1,1,256]{2,1,0:T(1,128)S(1)}, u32[]{:S(2)}, u32[]{:S(2)}) collective-permute-start(f32[1,1,256]{2,1,0:T(1,128)S(1)} %get-tuple-element.80), channel_id=1, source_target_pairs={{2,0},{4,2},{6,4},{8,6},{10,8},{12,10},{14,12},{0,14},{3,1},{5,3},... | collective-permute-start | bytes 3080 | tf_op jit(solution)/shard_map/ppermute | solution.py:22
  158.0 6.3 %collective-permute-start.24 = (f32[1,1,256]{2,1,0:T(1,128)S(1)}, f32[1,1,256]{2,1,0:T(1,128)S(1)}, u32[]{:S(2)}, u32[]{:S(2)}) collective-permute-start(f32[1,1,256]{2,1,0:T(1,128)S(1)} %get-tuple-element.77), channel_id=1, source_target_pairs={{0,2},{2,4},{4,6},{6,8},{8,10},{10,12},{12,14},{14,0},{1,3},{3,5},... | collective-permute-start | bytes 3080 | tf_op jit(solution)/shard_map/ppermute | solution.py:20
  158.1 6.3 %collective-permute-start.25 = (f32[1,1,256]{2,1,0:T(1,128)S(1)}, f32[1,1,256]{2,1,0:T(1,128)S(1)}, u32[]{:S(2)}, u32[]{:S(2)}) collective-permute-start(f32[1,1,256]{2,1,0:T(1,128)S(1)} %get-tuple-element.78), channel_id=1, source_target_pairs={{2,0},{4,2},{6,4},{8,6},{10,8},{12,10},{14,12},{0,14},{3,1},{5,3},... | collective-permute-start | bytes 3080 | tf_op jit(solution)/shard_map/ppermute | solution.py:22
  234.8 6.3 %collective-permute-start.28 = (f32[1,1,256]{2,1,0:T(1,128)S(1)}, f32[1,1,256]{2,1,0:T(1,128)S(1)}, u32[]{:S(2)}, u32[]{:S(2)}) collective-permute-start(f32[1,1,256]{2,1,0:T(1,128)S(1)} %get-tuple-element.75), channel_id=1, source_target_pairs={{0,2},{2,4},{4,6},{6,8},{8,10},{10,12},{12,14},{14,0},{1,3},{3,5},... | collective-permute-start | bytes 3080 | tf_op jit(solution)/shard_map/ppermute | solution.py:20
  234.9 6.3 %collective-permute-start.29 = (f32[1,1,256]{2,1,0:T(1,128)S(1)}, f32[1,1,256]{2,1,0:T(1,128)S(1)}, u32[]{:S(2)}, u32[]{:S(2)}) collective-permute-start(f32[1,1,256]{2,1,0:T(1,128)S(1)} %get-tuple-element.76), channel_id=1, source_target_pairs={{2,0},{4,2},{6,4},{8,6},{10,8},{12,10},{14,12},{0,14},{3,1},{5,3},... | collective-permute-start | bytes 3080 | tf_op jit(solution)/shard_map/ppermute | solution.py:22
  279.5 6.3 %collective-permute-start.32 = (f32[1,1,256]{2,1,0:T(1,128)S(1)}, f32[1,1,256]{2,1,0:T(1,128)S(1)}, u32[]{:S(2)}, u32[]{:S(2)}) collective-permute-start(f32[1,1,256]{2,1,0:T(1,128)S(1)} %get-tuple-element.73), channel_id=1, source_target_pairs={{0,2},{2,4},{4,6},{6,8},{8,10},{10,12},{12,14},{14,0},{1,3},{3,5},... | collective-permute-start | bytes 3080 | tf_op jit(solution)/shard_map/ppermute | solution.py:20
  279.6 6.3 %collective-permute-start.33 = (f32[1,1,256]{2,1,0:T(1,128)S(1)}, f32[1,1,256]{2,1,0:T(1,128)S(1)}, u32[]{:S(2)}, u32[]{:S(2)}) collective-permute-start(f32[1,1,256]{2,1,0:T(1,128)S(1)} %get-tuple-element.74), channel_id=1, source_target_pairs={{2,0},{4,2},{6,4},{8,6},{10,8},{12,10},{14,12},{0,14},{3,1},{5,3},... | collective-permute-start | bytes 3080 | tf_op jit(solution)/shard_map/ppermute | solution.py:22
  (48 other events, 586.9 us)
where the time goes:
time: 289 us; the launch traced here: 288 us
  blocking collectives  165 us (57%)
  starting transfers between devices  49.7 us (17%)
  other arithmetic  26.7 us (9%)
  local copies, waits for them, and re-layouts  23.8 us (8%)
  waiting for transfers between devices  15.4 us (5%)
  between operations  8.25 us (3%)
    psum x3, blocking collectives, total_norm(): return lax.psum(jnp.sum(field * field), ('gx', 'gy'))  95 us
    psum x2, blocking collectives, per_device(): step_size = norm_now / lax.psum(jnp.sum(direction * mapped), ('gx', 'gy'))  69.5 us
    ppermute x18, starting transfers between devices, extended(): lax.ppermute(head, axis, [((i + 1) % count, i) for i in range(count)])  45.5 us
    ppermute x18, waiting for transfers between devices, extended(): lax.ppermute(tail, axis, [(i, (i + 1) % count) for i in range(count)])  14.6 us
    concatenate x12, other arithmetic, extended(): jnp.concatenate([lax.ppermute(tail, axis, [(i, (i + 1) % count) for i in...  7.71 us
    slice x20, local copies, waits for them, and re-layouts, extended(): lax.slice_in_dim(cells, cells.shape[dim] - width, cells.shape[dim], axis=...  7.22 us
  transfers between devices with their start and end apart: 36, of which 17 were waited for; matrix products, arithmetic and copies ran while one was open for 5% of the time, Pallas kernels for 0%

commit v1 on v0

v1 whole, which is shorter than its diff:
```python
import functools

import jax
import jax.numpy as jnp
from jax import lax
from jax.experimental import pallas as pl
from jax.experimental.pallas import tpu as pltpu
from jax.sharding import PartitionSpec as P

SUB = 3
STIFFNESS = 0.1
MESH = pl.DeviceIdType.MESH


def kernel(
    count_x,
    tracer_in, east_in, north_in, flow_e, flow_n, mixing, buoyancy, coriolis,
    depth_in, adj_surface, surface_diag, prior,
    tracer_out, east_out, north_out, solution_out,
    rows_send, rows_recv,
    corner_send, corner_recv,
    side_recv,
    plane_rows_send, plane_rows_recv, plane_corner_recv, plane_side_send, plane_side_recv,
    sum_rows_send, sum_rows_recv, sum_corner_recv, sum_side_send, sum_side_recv,
    columns, moments,
    rows_ss, rows_rs, corner_ss, corner_rs, side_ss, side_rs,
    plane_ss, plane_rs, sum_ss, sum_rs, moment_ss, moment_rs,
):
    levels, cols, lanes = tracer_in.shape
    wide = lanes + 128
    tall = cols + 8
    group = lax.axis_index("groups")
    gx = lax.axis_index("gx")
    gy = lax.axis_index("gy")
    other = 1 - gy
    east_of = lax.rem(gx + 1, count_x)
    west_of = lax.rem(gx + count_x - 1, count_x)
    targets = (west_of, east_of)
    edge = pl.multiple_of(other * (lanes - 128), 128)
    me = gx * 2 + gy
    peers = 2 * count_x

    barrier = pltpu.get_barrier_semaphore()

    @pl.loop(1, peers)
    def _(step):
        peer = lax.rem(me + step, peers)
        pl.semaphore_signal(
            barrier, inc=1, device_id=(group, peer // 2, lax.rem(peer, 2)), device_id_type=MESH
        )

    sub8 = lax.broadcasted_iota(jnp.int32, (8, 1), 0)
    lane128 = lax.broadcasted_iota(jnp.int32, (1, 128), 1)

    def roll(x, shift, axis):
        return pltpu.roll(x, shift % x.shape[axis], axis)

    row = lax.broadcasted_iota(jnp.int32, (1, lanes), 1) + gy * lanes
    inside = ((row > 0) & (row < 2 * lanes - 1)).astype(jnp.float32)
    depth_own = depth_in[...].astype(jnp.float32) * inside
    planes = (depth_own, adj_surface[...], surface_diag[...], prior[...])

    def pack_pair(first, second, side):
        if side == 0:
            return jnp.where(sub8 < 4, first[:8], roll(second[:8], 4, 0))
        return jnp.where(sub8 >= 4, first[-8:], roll(second[-8:], 4, 0))

    for side in range(2):
        plane_rows_send[side, 0:8, :] = pack_pair(planes[0], planes[1], side)
        plane_rows_send[side, 8:16, :] = pack_pair(planes[2], planes[3], side)

    def edge_tile(x):
        return jnp.where(gy == 0, x[:, lanes - 128:], x[:, :128])

    for i, plane in enumerate(planes):
        plane_side_send[i] = edge_tile(plane)
    plane_side_send[4] = jnp.broadcast_to(edge_tile(coriolis[...]), (cols, 128))

    first_lane = other * 125
    edge_lane = (lane128 >= first_lane) & (lane128 < first_lane + 3)
    corner_send[...] = jnp.zeros_like(corner_send)

    def pack_three(first, second, two, k, side):
        if side == 0:
            a, b, c = first[k, 0:8, :], second[k, 0:8, :], two[k, 0:8, :]
            return jnp.where(sub8 < 3, a, jnp.where(sub8 < 6, roll(b, 3, 0), roll(c, 6, 0)))
        a, b, c = (r[k, cols - 8:cols, :] for r in (first, second, two))
        return jnp.where(sub8 >= 5, a, jnp.where(sub8 >= 2, roll(b, 5, 0), roll(c, 2, 0)))

    @pl.loop(0, levels)
    def _(k):
        for side in range(2):
            packed = jnp.concatenate(
                [
                    pack_three(tracer_in, east_in, flow_e, k, side),
                    pack_three(north_in, mixing, flow_n, k, side),
                ],
                axis=0,
            )
            rows_send[side, k] = packed
            tile = jnp.where(edge_lane, edge_tile(packed), 0.0)
            corner_send[side] = corner_send[side] + pltpu.roll(tile, 3 * k, 1)

    def remote(src, dst, ss, rs, x, y):
        return pltpu.make_async_remote_copy(
            src_ref=src, dst_ref=dst, send_sem=ss, recv_sem=rs,
            device_id=(group, x, y), device_id_type=MESH,
        )

    def planes_copies():
        out = [remote(plane_side_send, plane_side_recv, plane_ss.at[4], plane_rs.at[4], gx, other)]
        for side in range(2):
            out.append(remote(plane_rows_send.at[side], plane_rows_recv.at[side],
                              plane_ss.at[side], plane_rs.at[side], targets[side], gy))
            out.append(remote(plane_rows_send.at[side, :, pl.ds(edge, 128)], plane_corner_recv.at[side],
                              plane_ss.at[2 + side], plane_rs.at[2 + side], targets[side], other))
        return out

    def corner_copies():
        return [remote(corner_send.at[side], corner_recv.at[side], corner_ss.at[side],
                       corner_rs.at[side], targets[side], other) for side in range(2)]

    def side_copies():
        return [remote(ref.at[:, :, pl.ds(edge, 128)], side_recv.at[i], side_ss.at[i], side_rs.at[i], gx, other)
                for i, ref in enumerate((tracer_in, east_in, north_in, mixing, flow_e, flow_n))]

    def rows_copies(k):
        return [remote(rows_send.at[side, k], rows_recv.at[side, k], rows_ss.at[side, k],
                       rows_rs.at[side, k], targets[side], gy) for side in range(2)]

    def sums_copies():
        out = [remote(sum_side_send, sum_side_recv, sum_ss.at[4], sum_rs.at[4], gx, other)]
        for side in range(2):
            out.append(remote(sum_rows_send.at[side], sum_rows_recv.at[side],
                              sum_ss.at[side], sum_rs.at[side], targets[side], gy))
            out.append(remote(sum_rows_send.at[side, :, pl.ds(edge, 128)], sum_corner_recv.at[side],
                              sum_ss.at[2 + side], sum_rs.at[2 + side], targets[side], other))
        return out

    pl.semaphore_wait(barrier, peers - 1)
    for copy in planes_copies() + corner_copies() + side_copies():
        copy.start()

    @pl.loop(0, levels)
    def _(k):
        for copy in rows_copies(k):
            copy.start()

    columns[...] = jnp.zeros_like(columns)
    for copy in planes_copies() + corner_copies() + side_copies():
        copy.wait_recv()

    def to_east(x):
        return pltpu.roll(x, tall - 1, 0)

    def to_west(x):
        return pltpu.roll(x, 1, 0)

    def to_north(x):
        return pltpu.roll(x, wide - 1, 1)

    def to_south(x):
        return pltpu.roll(x, 1, 1)

    def assemble(own, side, halo):
        return jnp.concatenate([jnp.concatenate([own, side], axis=1), halo], axis=0)

    def halo_pair(rows, corner, first):
        e = jnp.concatenate([rows[0], corner[0]], axis=1)
        w = jnp.concatenate([rows[1], corner[1]], axis=1)
        both = jnp.where(sub8 < 4, e, w) if first else jnp.where(sub8 < 4, roll(e, 4, 0), roll(w, 4, 0))
        return both

    def plane_at(i):
        tile = slice(8 * (i // 2), 8 * (i // 2) + 8)
        halo = halo_pair(
            (plane_rows_recv[0, tile, :], plane_rows_recv[1, tile, :]),
            (plane_corner_recv[0, tile, :], plane_corner_recv[1, tile, :]),
            i % 2 == 0,
        )
        return assemble(planes[i], plane_side_recv[i], halo)

    depth = plane_at(0)
    rotation = jnp.concatenate([coriolis[...], plane_side_recv[4, 0:1, :]], axis=1)

    @pl.loop(0, levels)
    def _(k):
        for copy in rows_copies(k):
            copy.wait_recv()
        back = lax.rem(128 - 3 * k, 128)
        packed = [
            jnp.concatenate([rows_recv[side, k], pltpu.roll(corner_recv[side], back, 1)], axis=1)
            for side in range(2)
        ]

        def field(ref, i, tile, shift_e, shift_w):
            e = packed[0][8 * tile:8 * tile + 8]
            w = packed[1][8 * tile:8 * tile + 8]
            halo = jnp.where(sub8 < 4, roll(e, shift_e, 0), roll(w, shift_w, 0))
            return assemble(ref[k], side_recv[i, k], halo)

        wet = (k.astype(jnp.float32) < depth).astype(jnp.float32)
        wet_e, wet_n = to_east(wet) * wet, to_north(wet) * wet
        half_mix = 0.5 * field(mixing, 3, 1, 5, 3)
        face_e = (half_mix + to_east(half_mix)) * wet_e
        face_n = (half_mix + to_north(half_mix)) * wet_n
        face_w, face_s = to_west(face_e), to_south(face_n)
        half = 0.5 * wet
        carry_e = half * field(flow_e, 4, 0, 2, 6)
        carry_n = half * field(flow_n, 5, 1, 2, 6)
        take_e, take_w = face_e + carry_e, face_w - carry_e
        take_n, take_s = face_n + carry_n, face_s - carry_n
        take = wet - (face_e + face_w) - (face_n + face_s)
        turn = wet * rotation
        lift = buoyancy[k]
        lift_e, lift_n, lift_here = lift * wet_e, lift * wet_n, lift * wet
        t = wet * field(tracer_in, 0, 0, 0, 0)
        e = wet * field(east_in, 1, 0, 5, 3)
        n = wet * field(north_in, 2, 1, 0, 0)
        for _ in range(SUB):
            e_w, n_s = to_west(e), to_south(n)
            t_new = (take * t + take_e * to_east(t) + take_w * to_west(t)
                     + take_n * to_north(t) + take_s * to_south(t)
                     + (lift_e * e + lift_n * n - lift_here * (e_w + n_s)))
            e_new = (take * e + take_e * to_east(e) + take_w * e_w
                     + take_n * to_north(e) + take_s * to_south(e) - turn * n)
            n_new = (take * n + take_e * to_east(n) + take_w * to_west(n)
                     + take_n * to_north(n) + take_s * n_s + turn * e)
            t, e, n = t_new, e_new, n_new
        own = (slice(0, cols), slice(0, lanes))
        tracer_out[k] = t[own]
        east_out[k] = e[own]
        north_out[k] = n[own]
        columns[0] = columns[0] + e[own]
        columns[1] = columns[1] + n[own]

    sum_e, sum_n = columns[0], columns[1]
    for side in range(2):
        sum_rows_send[side] = pack_pair(sum_e, sum_n, side)
    sum_side_send[0] = edge_tile(sum_e)
    sum_side_send[1] = edge_tile(sum_n)
    for copy in sums_copies():
        copy.start()

    wet_column = (depth > 0.0).astype(jnp.float32)
    reach_e = STIFFNESS * jnp.minimum(depth, to_east(depth))
    reach_n = STIFFNESS * jnp.minimum(depth, to_north(depth))
    reach_w, reach_s = to_west(reach_e), to_south(reach_n)
    centre = plane_at(2) + (reach_e + reach_w) + (reach_n + reach_s)

    def operator(p):
        return (centre * p - reach_e * to_east(p) - reach_w * to_west(p)
                - reach_n * to_north(p) - reach_s * to_south(p))

    start = wet_column * plane_at(3)
    base = wet_column * plane_at(1) - operator(start)

    for copy in sums_copies():
        copy.wait_recv()

    def sum_at(i, own):
        halo = halo_pair((sum_rows_recv[0], sum_rows_recv[1]), (sum_corner_recv[0], sum_corner_recv[1]), i == 0)
        return assemble(own, sum_side_recv[i], halo)

    all_e, all_n = sum_at(0, sum_e), sum_at(1, sum_n)
    v0 = base + (0.5 * wet_column) * (to_west(all_e) - to_east(all_e) + to_south(all_n) - to_north(all_n))
    v1 = operator(v0)
    v2 = operator(v1)
    v3 = operator(v2)

    w = [v[0:cols, 0:lanes] for v in (v0, v1, v2, v3)]

    def partial(a, b):
        s = jnp.sum((a * b).reshape(cols // 8, 8, lanes), axis=0)
        total = s[:, 0:128]
        for j in range(128, lanes, 128):
            total = total + s[:, j:j + 128]
        return jnp.sum(total, axis=0, keepdims=True)

    terms = [partial(w[0], w[0]), partial(w[0], w[1]), partial(w[1], w[1]),
             partial(w[1], w[2]), partial(w[2], w[2]), partial(w[2], w[3])]
    mine = jnp.concatenate(terms + [jnp.zeros((2, 128), jnp.float32)], axis=0)
    moments[me] = mine

    def moment_copy(step):
        peer = lax.rem(me + step, peers)
        return remote(moments.at[me], moments.at[me], moment_ss.at[step], moment_rs.at[me],
                      peer // 2, lax.rem(peer, 2))

    @pl.loop(1, peers)
    def _(step):
        moment_copy(step).start()

    @pl.loop(1, peers)
    def _(step):
        source = lax.rem(me + step, peers)
        remote(moments.at[me], moments.at[source], moment_ss.at[step], moment_rs.at[source],
               source // 2, lax.rem(source, 2)).wait_recv()

    total = jnp.sum(jnp.sum(moments[...], axis=0), axis=1, keepdims=True)
    mu = [jnp.broadcast_to(total[m:m + 1, :], (1, 128)) for m in range(6)]

    def form(c, at):
        out = 0.0
        for i, a in enumerate(c):
            for j, b in enumerate(c):
                out = out + a * b * mu[at + i + j]
        return out

    r = [jnp.ones((1, 128), jnp.float32)]
    d = list(r)
    rr = mu[0]
    gain = [jnp.zeros((1, 128), jnp.float32) for _ in range(3)]
    for iteration in range(3):
        alpha = rr / form(d, 1)
        for i in range(len(d)):
            gain[i] = gain[i] + alpha * d[i]
        if iteration < 2:
            shifted = [jnp.zeros((1, 128), jnp.float32)] + d
            r = [a - alpha * b for a, b in zip(r + [jnp.zeros((1, 128), jnp.float32)], shifted)]
            new = form(r, 0)
            beta = new / rr
            d = [a + beta * b for a, b in zip(r, d + [jnp.zeros((1, 128), jnp.float32)])]
            rr = new
    gain = [g[:, 0:1] for g in gain]
    solved = start + gain[0] * v0 + gain[1] * v1 + gain[2] * v2
    solution_out[...] = solved[0:cols, 0:lanes]
    grad_e = (0.5 * (to_east(solved) - to_west(solved)))[0:cols, 0:lanes]
    grad_n = (0.5 * (to_north(solved) - to_south(solved)))[0:cols, 0:lanes]

    @pl.loop(0, levels)
    def _(k):
        wet = k.astype(jnp.float32) < depth_own
        east_out[k] = east_out[k] + jnp.where(wet, grad_e, 0.0)
        north_out[k] = north_out[k] + jnp.where(wet, grad_n, 0.0)

    for copy in planes_copies() + corner_copies() + side_copies() + sums_copies():
        copy.wait_send()

    @pl.loop(0, levels)
    def _(k):
        for copy in rows_copies(k):
            copy.wait_send()

    @pl.loop(1, peers)
    def _(step):
        moment_copy(step).wait_send()


def per_device(count_x, *args):
    levels, cols, lanes = args[0].shape
    args = list(args)
    args[7] = args[7].reshape(1, lanes)
    f32 = jnp.float32
    vmem = pl.BlockSpec(memory_space=pltpu.VMEM)
    specs = [vmem] * 12
    specs[6] = pl.BlockSpec(memory_space=pltpu.SMEM)
    peers = 2 * count_x
    dma = pltpu.SemaphoreType.DMA
    scratch = [
        pltpu.VMEM((2, levels, 16, lanes), f32), pltpu.VMEM((2, levels, 16, lanes), f32),
        pltpu.VMEM((2, 16, 128), f32), pltpu.VMEM((2, 16, 128), f32),
        pltpu.VMEM((6, levels, cols, 128), f32),
        pltpu.VMEM((2, 16, lanes), f32), pltpu.VMEM((2, 16, lanes), f32), pltpu.VMEM((2, 16, 128), f32),
        pltpu.VMEM((5, cols, 128), f32), pltpu.VMEM((5, cols, 128), f32),
        pltpu.VMEM((2, 8, lanes), f32), pltpu.VMEM((2, 8, lanes), f32), pltpu.VMEM((2, 8, 128), f32),
        pltpu.VMEM((2, cols, 128), f32), pltpu.VMEM((2, cols, 128), f32),
        pltpu.VMEM((2, cols, lanes), f32), pltpu.VMEM((peers, 8, 128), f32),
        dma((2, levels)), dma((2, levels)), dma((2,)), dma((2,)), dma((6,)), dma((6,)),
        dma((5,)), dma((5,)), dma((5,)), dma((5,)), dma((peers,)), dma((peers,)),
    ]
    volume = jax.ShapeDtypeStruct((levels, cols, lanes), f32)
    return pl.pallas_call(
        functools.partial(kernel, count_x),
        out_shape=[volume] * 3 + [jax.ShapeDtypeStruct((cols, lanes), f32)],
        in_specs=specs,
        out_specs=[vmem] * 4,
        scratch_shapes=scratch,
        compiler_params=pltpu.CompilerParams(
            collective_id=0, has_side_effects=True, vmem_limit_bytes=32 * 1024 * 1024
        ),
    )(*args)


def solution(mesh):
    volume = P("groups", "gx", "gy")
    plane = P(("groups", "gx"), "gy")
    return jax.shard_map(
        functools.partial(per_device, mesh.shape["gx"]),
        mesh=mesh,
        in_specs=(volume,) * 6 + (P(), P("gy")) + (plane,) * 4,
        out_specs=(volume,) * 3 + (plane,),
        check_vma=False,
    )
```

time: 289 us -> 43.1 us (0.15)
  blocking collectives: 165 us -> 0 us
  starting transfers between devices: 49.7 us -> 0 us
  Pallas kernels: 0 us -> 29.5 us
  other arithmetic: 26.7 us -> 0 us
  waiting for transfers between devices: 15.4 us -> 0 us
  local copies, waits for them, and re-layouts: 23.8 us -> 12.3 us
  between operations: 8.25 us -> 0.67 us
    psum x5 -> x0, blocking collectives: 165 us -> none  [the longest x3 95 us: total_norm(): return lax.psum(jnp.sum(field * field), ('gx', 'gy'))]
    ppermute x36 -> x0, starting transfers between devices: 49.7 us -> none  [the longest x18 45.5 us: extended(): lax.ppermute(head, axis, [((i + 1) % count, i) for i in range(count)])]
    pallas_call x0 -> x1, Pallas kernels: none -> 29.5 us  [per_device(): pl.pallas_call(functools.partial(kernel, count_x), out_shape=[volume] * 3...]
    ppermute x36 -> x0, waiting for transfers between devices: 15.4 us -> none  [the longest x18 14.6 us: extended(): lax.ppermute(tail, axis, [(i, (i + 1) % count) for i in range(count)])]
    slice x25 -> x0, local copies, waits for them, and re-layouts: 11.4 us -> none  [the longest x20 7.22 us: extended(): lax.slice_in_dim(cells, cells.shape[dim] - width, cells.shape[dim], axis=...]
    ppermute x8 -> x0, local copies, waits for them, and re-layouts: 9.98 us -> none  [the longest x4 5.42 us: extended(): lax.ppermute(head, axis, [((i + 1) % count, i) for i in range(count)])]
    unnamed x76 -> x28, local copies, waits for them, and re-layouts: 2.39 us -> 12.3 us
    concatenate x12 -> x0, other arithmetic: 7.71 us -> none  [extended(): jnp.concatenate([lax.ppermute(tail, axis, [(i, (i + 1) % count) for i in...]
  transfers between devices with their start and end apart: 36 -> 0, of which waited for: 17 -> 0; matrix products, arithmetic and copies ran while one was open for 5% -> 0% of each run, Pallas kernels for 0% -> 0%
where the time goes in v1:
time: 43.1 us; the launch traced here: 42.5 us
  Pallas kernels  29.5 us (68%)
  local copies, waits for them, and re-layouts  12.3 us (29%)
  between operations  0.67 us (2%)
    pallas_call x1, Pallas kernels, per_device(): pl.pallas_call(functools.partial(kernel, count_x), out_shape=[volume] * 3...  29.5 us
    unnamed x28, local copies, waits for them, and re-layouts  12.3 us

profile of v1, /device:TPU:0, one launch (start us, length us, event | category | flops | bytes accessed | tf_op | source)
XLA Modules:
  0.0 42.5 jit_solution(15984504309645265301)
XLA Ops:
  0.6 0.0 copy-start.10
  0.6 0.0 copy-start.11
  0.7 0.7 %copy-done.10 = f32[256]{0:T(256)S(1)} copy-done((f32[256]{0:T(256)S(1)}, f32[256]{0:T(256)}, u32[]{:S(2)}) %copy-start.10) | copy-done | bytes 1048
  1.3 0.0 copy-done.11
  1.3 0.0 copy-start
  1.3 1.0 %copy-done = f32[10,32,256]{2,1,0:T(8,128)S(1)} copy-done((f32[10,32,256]{2,1,0:T(8,128)S(1)}, f32[10,32,256]{2,1,0:T(8,128)}, u32[]{:S(2)}) %copy-start) | copy-done | bytes 327704
  2.3 0.0 copy-start.1
  2.3 1.0 %copy-done.1 = f32[10,32,256]{2,1,0:T(8,128)S(1)} copy-done((f32[10,32,256]{2,1,0:T(8,128)S(1)}, f32[10,32,256]{2,1,0:T(8,128)}, u32[]{:S(2)}) %copy-start.1) | copy-done | bytes 327704
  3.3 0.0 copy-start.2
  3.3 1.0 %copy-done.2 = f32[10,32,256]{2,1,0:T(8,128)S(1)} copy-done((f32[10,32,256]{2,1,0:T(8,128)S(1)}, f32[10,32,256]{2,1,0:T(8,128)}, u32[]{:S(2)}) %copy-start.2) | copy-done | bytes 327704
  4.2 0.0 copy-start.3
  4.2 1.0 %copy-done.3 = f32[10,32,256]{2,1,0:T(8,128)S(1)} copy-done((f32[10,32,256]{2,1,0:T(8,128)S(1)}, f32[10,32,256]{2,1,0:T(8,128)}, u32[]{:S(2)}) %copy-start.3) | copy-done | bytes 327704
  5.2 0.0 copy-start.4
  5.2 1.0 %copy-done.4 = f32[10,32,256]{2,1,0:T(8,128)S(1)} copy-done((f32[10,32,256]{2,1,0:T(8,128)S(1)}, f32[10,32,256]{2,1,0:T(8,128)}, u32[]{:S(2)}) %copy-start.4) | copy-done | bytes 327704
  6.2 1.0 %copy-done.5 = f32[10,32,256]{2,1,0:T(8,128)S(1)} copy-done((f32[10,32,256]{2,1,0:T(8,128)S(1)}, f32[10,32,256]{2,1,0:T(8,128)}, u32[]{:S(2)}) %copy-start.5) | copy-done | bytes 327704
  7.2 0.8 %copy-done.6 = s32[32,256]{1,0:T(8,128)S(1)} copy-done((s32[32,256]{1,0:T(8,128)S(1)}, s32[32,256]{1,0:T(8,128)}, u32[]{:S(2)}) %copy-start.6) | copy-done | bytes 32792
  7.9 0.8 %copy-done.7 = f32[32,256]{1,0:T(8,128)S(1)} copy-done((f32[32,256]{1,0:T(8,128)S(1)}, f32[32,256]{1,0:T(8,128)}, u32[]{:S(2)}) %copy-start.7) | copy-done | bytes 32792
  8.7 0.8 %copy-done.8 = f32[32,256]{1,0:T(8,128)S(1)} copy-done((f32[32,256]{1,0:T(8,128)S(1)}, f32[32,256]{1,0:T(8,128)}, u32[]{:S(2)}) %copy-start.8) | copy-done | bytes 32792
  9.4 0.8 %copy-done.9 = f32[32,256]{1,0:T(8,128)S(1)} copy-done((f32[32,256]{1,0:T(8,128)S(1)}, f32[32,256]{1,0:T(8,128)}, u32[]{:S(2)}) %copy-start.9) | copy-done | bytes 32792
  10.2 29.5 %shard_map.147 = (f32[10,32,256]{2,1,0:T(8,128)S(1)}, f32[10,32,256]{2,1,0:T(8,128)S(1)}, f32[10,32,256]{2,1,0:T(8,128)S(1)}, f32[32,256]{1,0:T(8,128)S(1)}) custom-call(f32[10,32,256]{2,1,0:T(8,128)S(1)} %copy-done, f32[10,32,256]{2,1,0:T(8,128)S(1)} %copy-done.1, f32[10,32,256]{2,1,0:T(8,128)S(1)} %copy-done.2, f32[10,32,256]{2,1,0:T(8,128)S(1)} %copy-done.3, ...), custom_call_target="tpu_custom_call" | custom-call | tf_op jit(solution)/shard_map/pallas_call | solution.py:373
  39.7 0.7 %copy.20 = f32[10,32,256]{2,1,0:T(8,128)} copy(f32[10,32,256]{2,1,0:T(8,128)S(1)} %get-tuple-element.8) | data formatting | bytes 655360
  40.4 0.7 %copy.21 = f32[10,32,256]{2,1,0:T(8,128)} copy(f32[10,32,256]{2,1,0:T(8,128)S(1)} %get-tuple-element.9) | data formatting | bytes 655360
  41.2 0.7 %copy.22 = f32[10,32,256]{2,1,0:T(8,128)} copy(f32[10,32,256]{2,1,0:T(8,128)S(1)} %get-tuple-element.10) | data formatting | bytes 655360
  41.9 0.6 %copy.23 = f32[32,256]{1,0:T(8,128)} copy(f32[32,256]{1,0:T(8,128)S(1)} %get-tuple-element.11) | data formatting | bytes 65536
  (5 shorter events, 0.0 us)
Async XLA Ops:
  0.6 0.7 %copy-start.10 = (f32[256]{0:T(256)S(1)}, f32[256]{0:T(256)}, u32[]{:S(2)}) copy-start(f32[256]{0:T(256)} %param.19) | copy-start | bytes 3076
  0.6 0.7 %copy-start.11 = (f32[10]{0:T(128)S(1)}, f32[10]{0:T(128)}, u32[]{:S(2)}) copy-start(f32[10]{0:T(128)} %buoyancy.1) | copy-start | bytes 124
  1.3 1.0 %copy-start = (f32[10,32,256]{2,1,0:T(8,128)S(1)}, f32[10,32,256]{2,1,0:T(8,128)}, u32[]{:S(2)}) copy-start(f32[10,32,256]{2,1,0:T(8,128)} %tracer_in.1) | copy-start | bytes 983044
  2.3 1.0 %copy-start.1 = (f32[10,32,256]{2,1,0:T(8,128)S(1)}, f32[10,32,256]{2,1,0:T(8,128)}, u32[]{:S(2)}) copy-start(f32[10,32,256]{2,1,0:T(8,128)} %east_in.1) | copy-start | bytes 983044
  3.3 1.0 %copy-start.2 = (f32[10,32,256]{2,1,0:T(8,128)S(1)}, f32[10,32,256]{2,1,0:T(8,128)}, u32[]{:S(2)}) copy-start(f32[10,32,256]{2,1,0:T(8,128)} %north_in.1) | copy-start | bytes 983044
  4.2 1.0 %copy-start.3 = (f32[10,32,256]{2,1,0:T(8,128)S(1)}, f32[10,32,256]{2,1,0:T(8,128)}, u32[]{:S(2)}) copy-start(f32[10,32,256]{2,1,0:T(8,128)} %flow_e.1) | copy-start | bytes 983044
  5.2 1.0 %copy-start.4 = (f32[10,32,256]{2,1,0:T(8,128)S(1)}, f32[10,32,256]{2,1,0:T(8,128)}, u32[]{:S(2)}) copy-start(f32[10,32,256]{2,1,0:T(8,128)} %flow_n.1) | copy-start | bytes 983044
  6.2 1.0 %copy-start.5 = (f32[10,32,256]{2,1,0:T(8,128)S(1)}, f32[10,32,256]{2,1,0:T(8,128)}, u32[]{:S(2)}) copy-start(f32[10,32,256]{2,1,0:T(8,128)} %mixing.1) | copy-start | bytes 983044
  7.2 0.8 %copy-start.6 = (s32[32,256]{1,0:T(8,128)S(1)}, s32[32,256]{1,0:T(8,128)}, u32[]{:S(2)}) copy-start(s32[32,256]{1,0:T(8,128)} %depth_in.1) | copy-start | bytes 98308
  7.9 0.8 %copy-start.7 = (f32[32,256]{1,0:T(8,128)S(1)}, f32[32,256]{1,0:T(8,128)}, u32[]{:S(2)}) copy-start(f32[32,256]{1,0:T(8,128)} %adj_surface.1) | copy-start | bytes 98308
  8.7 0.8 %copy-start.8 = (f32[32,256]{1,0:T(8,128)S(1)}, f32[32,256]{1,0:T(8,128)}, u32[]{:S(2)}) copy-start(f32[32,256]{1,0:T(8,128)} %surface_diag.1) | copy-start | bytes 98308
  9.4 0.8 %copy-start.9 = (f32[32,256]{1,0:T(8,128)S(1)}, f32[32,256]{1,0:T(8,128)}, u32[]{:S(2)}) copy-start(f32[32,256]{1,0:T(8,128)} %prior.1) | copy-start | bytes 98308

commit v2 on v1

--- a/solution.py
+++ b/solution.py
@@ -14,15 +14,17 @@
 
 def kernel(
     count_x,
+    tracer_hbm, east_hbm, north_hbm, flow_e_hbm, flow_n_hbm, mixing_hbm, buoyancy_hbm, coriolis_hbm,
+    depth_hbm, adj_surface_hbm, surface_diag_hbm, prior_hbm,
+    tracer_out, east_out, north_out, solution_out, grad_e_out, grad_n_out, depth_out,
     tracer_in, east_in, north_in, flow_e, flow_n, mixing, buoyancy, coriolis,
     depth_in, adj_surface, surface_diag, prior,
-    tracer_out, east_out, north_out, solution_out,
     rows_send, rows_recv,
     corner_send, corner_recv,
     side_recv,
     plane_rows_send, plane_rows_recv, plane_corner_recv, plane_side_send, plane_side_recv,
     sum_rows_send, sum_rows_recv, sum_corner_recv, sum_side_send, sum_side_recv,
-    columns, moments,
+    columns, moments, load_sem,
     rows_ss, rows_rs, corner_ss, corner_rs, side_ss, side_rs,
     plane_ss, plane_rs, sum_ss, sum_rs, moment_ss, moment_rs,
 ):
@@ -40,6 +42,21 @@
     me = gx * 2 + gy
     peers = 2 * count_x
 
+    fields_hbm = (tracer_hbm, east_hbm, north_hbm, mixing_hbm, flow_e_hbm, flow_n_hbm)
+    small = [
+        pltpu.make_async_copy(src, dst, load_sem.at[i])
+        for i, (src, dst) in enumerate([
+            (depth_hbm, depth_in), (adj_surface_hbm, adj_surface), (surface_diag_hbm, surface_diag),
+            (prior_hbm, prior), (coriolis_hbm, coriolis), (buoyancy_hbm, buoyancy),
+        ])
+    ]
+    large = [
+        pltpu.make_async_copy(src, dst, load_sem.at[6 + i])
+        for i, (src, dst) in enumerate(zip(fields_hbm, (tracer_in, east_in, north_in, mixing, flow_e, flow_n)))
+    ]
+    for copy in small + large:
+        copy.start()
+
     barrier = pltpu.get_barrier_semaphore()
 
     @pl.loop(1, peers)
@@ -55,6 +72,9 @@
     def roll(x, shift, axis):
         return pltpu.roll(x, shift % x.shape[axis], axis)
 
+    for copy in small:
+        copy.wait()
+
     row = lax.broadcasted_iota(jnp.int32, (1, lanes), 1) + gy * lanes
     inside = ((row > 0) & (row < 2 * lanes - 1)).astype(jnp.float32)
     depth_own = depth_in[...].astype(jnp.float32) * inside
@@ -86,6 +106,48 @@
             return jnp.where(sub8 < 3, a, jnp.where(sub8 < 6, roll(b, 3, 0), roll(c, 6, 0)))
         a, b, c = (r[k, cols - 8:cols, :] for r in (first, second, two))
         return jnp.where(sub8 >= 5, a, jnp.where(sub8 >= 2, roll(b, 5, 0), roll(c, 2, 0)))
+
+    def remote(src, dst, ss, rs, x, y):
+        return pltpu.make_async_remote_copy(
+            src_ref=src, dst_ref=dst, send_sem=ss, recv_sem=rs,
+            device_id=(group, x, y), device_id_type=MESH,
+        )
+
+    def planes_copies():
+        out = [remote(plane_side_send, plane_side_recv, plane_ss.at[4], plane_rs.at[4], gx, other)]
+        for side in range(2):
+            out.append(remote(plane_rows_send.at[side], plane_rows_recv.at[side],
+                              plane_ss.at[side], plane_rs.at[side], targets[side], gy))
+            out.append(remote(plane_rows_send.at[side, :, pl.ds(edge, 128)], plane_corner_recv.at[side],
+                              plane_ss.at[2 + side], plane_rs.at[2 + side], targets[side], other))
+        return out
+
+    def corner_copies():
+        return [remote(corner_send.at[side], corner_recv.at[side], corner_ss.at[side],
+                       corner_rs.at[side], targets[side], other) for side in range(2)]
+
+    def side_copies():
+        return [remote(ref.at[:, :, pl.ds(edge, 128)], side_recv.at[i], side_ss.at[i], side_rs.at[i], gx, other)
+                for i, ref in enumerate(fields_hbm)]
+
+    def rows_copies(k):
+        return [remote(rows_send.at[side, k], rows_recv.at[side, k], rows_ss.at[side, k],
+                       rows_rs.at[side, k], targets[side], gy) for side in range(2)]
+
+    def sums_copies():
+        out = [remote(sum_side_send, sum_side_recv, sum_ss.at[4], sum_rs.at[4], gx, other)]
+        for side in range(2):
+            out.append(remote(sum_rows_send.at[side], sum_rows_recv.at[side],
+                              sum_ss.at[side], sum_rs.at[side], targets[side], gy))
+            out.append(remote(sum_rows_send.at[side, :, pl.ds(edge, 128)], sum_corner_recv.at[side],
+                              sum_ss.at[2 + side], sum_rs.at[2 + side], targets[side], other))
+        return out
+
+    pl.semaphore_wait(barrier, peers - 1)
+    for copy in planes_copies() + side_copies():
+        copy.start()
+    for copy in large:
+        copy.wait()
 
     @pl.loop(0, levels)
     def _(k):
@@ -100,51 +162,11 @@
             rows_send[side, k] = packed
             tile = jnp.where(edge_lane, edge_tile(packed), 0.0)
             corner_send[side] = corner_send[side] + pltpu.roll(tile, 3 * k, 1)
-
-    def remote(src, dst, ss, rs, x, y):
-        return pltpu.make_async_remote_copy(
-            src_ref=src, dst_ref=dst, send_sem=ss, recv_sem=rs,
-            device_id=(group, x, y), device_id_type=MESH,
-        )
-
-    def planes_copies():
-        out = [remote(plane_side_send, plane_side_recv, plane_ss.at[4], plane_rs.at[4], gx, other)]
-        for side in range(2):
-            out.append(remote(plane_rows_send.at[side], plane_rows_recv.at[side],
-                              plane_ss.at[side], plane_rs.at[side], targets[side], gy))
-            out.append(remote(plane_rows_send.at[side, :, pl.ds(edge, 128)], plane_corner_recv.at[side],
-                              plane_ss.at[2 + side], plane_rs.at[2 + side], targets[side], other))
-        return out
-
-    def corner_copies():
-        return [remote(corner_send.at[side], corner_recv.at[side], corner_ss.at[side],
-                       corner_rs.at[side], targets[side], other) for side in range(2)]
-
-    def side_copies():
-        return [remote(ref.at[:, :, pl.ds(edge, 128)], side_recv.at[i], side_ss.at[i], side_rs.at[i], gx, other)
-                for i, ref in enumerate((tracer_in, east_in, north_in, mixing, flow_e, flow_n))]
-
-    def rows_copies(k):
-        return [remote(rows_send.at[side, k], rows_recv.at[side, k], rows_ss.at[side, k],
-                       rows_rs.at[side, k], targets[side], gy) for side in range(2)]
-
-    def sums_copies():
-        out = [remote(sum_side_send, sum_side_recv, sum_ss.at[4], sum_rs.at[4], gx, other)]
-        for side in range(2):
-            out.append(remote(sum_rows_send.at[side], sum_rows_recv.at[side],
-                              sum_ss.at[side], sum_rs.at[side], targets[side], gy))
-            out.append(remote(sum_rows_send.at[side, :, pl.ds(edge, 128)], sum_corner_recv.at[side],
-                              sum_ss.at[2 + side], sum_rs.at[2 + side], targets[side], other))
-        return out
-
-    pl.semaphore_wait(barrier, peers - 1)
-    for copy in planes_copies() + corner_copies() + side_copies():
-        copy.start()
-
-    @pl.loop(0, levels)
-    def _(k):
         for copy in rows_copies(k):
             copy.start()
+
+    for copy in corner_copies():
+        copy.start()
 
     columns[...] = jnp.zeros_like(columns)
     for copy in planes_copies() + corner_copies() + side_copies():
@@ -325,14 +347,9 @@
     gain = [g[:, 0:1] for g in gain]
     solved = start + gain[0] * v0 + gain[1] * v1 + gain[2] * v2
     solution_out[...] = solved[0:cols, 0:lanes]
-    grad_e = (0.5 * (to_east(solved) - to_west(solved)))[0:cols, 0:lanes]
-    grad_n = (0.5 * (to_north(solved) - to_south(solved)))[0:cols, 0:lanes]
-
-    @pl.loop(0, levels)
-    def _(k):
-        wet = k.astype(jnp.float32) < depth_own
-        east_out[k] = east_out[k] + jnp.where(wet, grad_e, 0.0)
-        north_out[k] = north_out[k] + jnp.where(wet, grad_n, 0.0)
+    grad_e_out[...] = (0.5 * (to_east(solved) - to_west(solved)))[0:cols, 0:lanes]
+    grad_n_out[...] = (0.5 * (to_north(solved) - to_south(solved)))[0:cols, 0:lanes]
+    depth_out[...] = depth_own
 
     for copy in planes_copies() + corner_copies() + side_copies() + sums_copies():
         copy.wait_send()
@@ -353,11 +370,12 @@
     args[7] = args[7].reshape(1, lanes)
     f32 = jnp.float32
     vmem = pl.BlockSpec(memory_space=pltpu.VMEM)
-    specs = [vmem] * 12
-    specs[6] = pl.BlockSpec(memory_space=pltpu.SMEM)
+    hbm = pl.BlockSpec(memory_space=pltpu.HBM)
     peers = 2 * count_x
     dma = pltpu.SemaphoreType.DMA
-    scratch = [
+    scratch = [pltpu.VMEM((levels, cols, lanes), f32)] * 6 + [
+        pltpu.SMEM((levels,), f32), pltpu.VMEM((1, lanes), f32), pltpu.VMEM((cols, lanes), args[8].dtype),
+    ] + [pltpu.VMEM((cols, lanes), f32)] * 3 + [
         pltpu.VMEM((2, levels, 16, lanes), f32), pltpu.VMEM((2, levels, 16, lanes), f32),
         pltpu.VMEM((2, 16, 128), f32), pltpu.VMEM((2, 16, 128), f32),
         pltpu.VMEM((6, levels, cols, 128), f32),
@@ -365,21 +383,24 @@
         pltpu.VMEM((5, cols, 128), f32), pltpu.VMEM((5, cols, 128), f32),
         pltpu.VMEM((2, 8, lanes), f32), pltpu.VMEM((2, 8, lanes), f32), pltpu.VMEM((2, 8, 128), f32),
         pltpu.VMEM((2, cols, 128), f32), pltpu.VMEM((2, cols, 128), f32),
-        pltpu.VMEM((2, cols, lanes), f32), pltpu.VMEM((peers, 8, 128), f32),
+        pltpu.VMEM((2, cols, lanes), f32), pltpu.VMEM((peers, 8, 128), f32), dma((12,)),
         dma((2, levels)), dma((2, levels)), dma((2,)), dma((2,)), dma((6,)), dma((6,)),
         dma((5,)), dma((5,)), dma((5,)), dma((5,)), dma((peers,)), dma((peers,)),
     ]
     volume = jax.ShapeDtypeStruct((levels, cols, lanes), f32)
-    return pl.pallas_call(
+    plane = jax.ShapeDtypeStruct((cols, lanes), f32)
+    tracer, east, north, solved, grad_e, grad_n, depth = pl.pallas_call(
         functools.partial(kernel, count_x),
-        out_shape=[volume] * 3 + [jax.ShapeDtypeStruct((cols, lanes), f32)],
-        in_specs=specs,
-        out_specs=[vmem] * 4,
+        out_shape=[volume] * 3 + [plane] * 4,
+        in_specs=[hbm] * 12,
+        out_specs=[vmem] * 7,
         scratch_shapes=scratch,
         compiler_params=pltpu.CompilerParams(
-            collective_id=0, has_side_effects=True, vmem_limit_bytes=32 * 1024 * 1024
+            collective_id=0, has_side_effects=True, vmem_limit_bytes=60 * 1024 * 1024
         ),
     )(*args)
+    wet = (jnp.arange(levels, dtype=f32)[:, None, None] < depth[None]).astype(f32)
+    return wet * tracer, east + wet * grad_e, north + wet * grad_n, solved
 
 
 def solution(mesh):

time: 43.1 us -> 36.1 us (0.84); the launches traced: 42.5 us -> 36 us
  local copies, waits for them, and re-layouts: 12.3 us -> 0.62 us
  Pallas kernels: 29.5 us -> 32.5 us
  other arithmetic: 0 us -> 2.21 us
    unnamed x28 -> x3, local copies, waits for them, and re-layouts: 12.3 us -> 0.62 us
    pallas_call x1, Pallas kernels: 29.5 us -> 32.5 us  [per_device(): pl.pallas_call(functools.partial(kernel, count_x), out_shape=[volume] * 3...]
    add x0 -> x1, other arithmetic: none -> 2.21 us  [per_device(): return (wet * tracer, east + wet * grad_e, north + wet * grad_n, solved)]
where the time goes in v2:
time: 36.1 us; the launch traced here: 36 us
  Pallas kernels  32.5 us (90%)
  other arithmetic  2.21 us (6%)
  between operations  0.65 us (2%)
  local copies, waits for them, and re-layouts  0.62 us (2%)
    pallas_call x1, Pallas kernels, per_device(): pl.pallas_call(functools.partial(kernel, count_x), out_shape=[volume] * 3...  32.5 us
    add x1, other arithmetic, per_device(): return (wet * tracer, east + wet * grad_e, north + wet * grad_n, solved)  2.21 us

profile of v2, /device:TPU:0, one launch (start us, length us, event | category | flops | bytes accessed | tf_op | source)
XLA Modules:
  0.0 36.0 jit_solution(15180943870739826393)
XLA Ops:
  0.6 32.5 %shard_map.147 = (f32[10,32,256]{2,1,0:T(8,128)}, f32[10,32,256]{2,1,0:T(8,128)}, f32[10,32,256]{2,1,0:T(8,128)}, f32[32,256]{1,0:T(8,128)}, f32[32,256]{1,0:T(8...) custom-call(f32[10,32,256]{2,1,0:T(8,128)} %tracer_hbm.1, f32[10,32,256]{2,1,0:T(8,128)} %east_hbm.1, ...), custom_call_target="tpu_custom_call" | custom-call | tf_op jit(solution)/shard_map/pallas_call | solution.py:392
  33.1 0.0 copy-start
  33.1 2.2 %select_add_fusion = (f32[10,32,256]{2,1,0:T(8,128)}, f32[10,32,256]{2,1,0:T(8,128)}, f32[10,32,256]{2,1,0:T(8,128)}) fusion(f32[10,32,256]{2,1,0:T(8,128)} %get-tuple-element.15, f32[32,256]{1,0:T(8,128)} %get-tuple-element.16, f32[32,256]{1,0:T(8,128)} %get-tuple-element.11, f32[10,32,256]{2,1,0:T(8,128)} %get-tuple-element.13, ...), kind=kLoop, calls=%fused_computation | loop fusion | flops 491520 | bytes 2064384 | tf_op jit(solution)/shard_map/add | solution.py:403
  35.4 0.0 copy-done
  35.4 0.6 %copy.17 = f32[32,256]{1,0:T(8,128)} copy(f32[32,256]{1,0:T(8,128)S(1)} %copy-done) | data formatting | bytes 65536
Async XLA Ops:
  33.1 2.2 %copy-start = (f32[32,256]{1,0:T(8,128)S(1)}, f32[32,256]{1,0:T(8,128)}, u32[]{:S(2)}) copy-start(f32[32,256]{1,0:T(8,128)} %get-tuple-element.28) | copy-start | bytes 98308

commit v3 on v2

--- a/solution.py
+++ b/solution.py
@@ -9,6 +9,7 @@
 
 SUB = 3
 STIFFNESS = 0.1
+WINDOW = 6
 MESH = pl.DeviceIdType.MESH
 
 
@@ -41,6 +42,16 @@
     edge = pl.multiple_of(other * (lanes - 128), 128)
     me = gx * 2 + gy
     peers = 2 * count_x
+    window = min(WINDOW, levels)
+
+    barrier = pltpu.get_barrier_semaphore()
+
+    @pl.loop(1, peers)
+    def _(step):
+        peer = lax.rem(me + step, peers)
+        pl.semaphore_signal(
+            barrier, inc=1, device_id=(group, peer // 2, lax.rem(peer, 2)), device_id_type=MESH
+        )
 
     fields_hbm = (tracer_hbm, east_hbm, north_hbm, mixing_hbm, flow_e_hbm, flow_n_hbm)
     small = [
@@ -57,15 +68,6 @@
     for copy in small + large:
         copy.start()
 
-    barrier = pltpu.get_barrier_semaphore()
-
-    @pl.loop(1, peers)
-    def _(step):
-        peer = lax.rem(me + step, peers)
-        pl.semaphore_signal(
-            barrier, inc=1, device_id=(group, peer // 2, lax.rem(peer, 2)), device_id_type=MESH
-        )
-
     sub8 = lax.broadcasted_iota(jnp.int32, (8, 1), 0)
     lane128 = lax.broadcasted_iota(jnp.int32, (1, 128), 1)
 
@@ -162,11 +164,14 @@
             rows_send[side, k] = packed
             tile = jnp.where(edge_lane, edge_tile(packed), 0.0)
             corner_send[side] = corner_send[side] + pltpu.roll(tile, 3 * k, 1)
+
+    for copy in corner_copies():
+        copy.start()
+
+    @pl.loop(0, window)
+    def _(k):
         for copy in rows_copies(k):
             copy.start()
-
-    for copy in corner_copies():
-        copy.start()
 
     columns[...] = jnp.zeros_like(columns)
     for copy in planes_copies() + corner_copies() + side_copies():
@@ -209,6 +214,14 @@
     def _(k):
         for copy in rows_copies(k):
             copy.wait_recv()
+
+        @pl.when(k + window < levels)
+        def _():
+            for copy in rows_copies(k):
+                copy.wait_send()
+            for copy in rows_copies(k + window):
+                copy.start()
+
         back = lax.rem(128 - 3 * k, 128)
         packed = [
             jnp.concatenate([rows_recv[side, k], pltpu.roll(corner_recv[side], back, 1)], axis=1)
@@ -354,7 +367,7 @@
     for copy in planes_copies() + corner_copies() + side_copies() + sums_copies():
         copy.wait_send()
 
-    @pl.loop(0, levels)
+    @pl.loop(levels - window, levels)
     def _(k):
         for copy in rows_copies(k):
             copy.wait_send()

time: 36.1 us -> 32.4 us (0.90)
  Pallas kernels: 32.5 us -> 28.8 us
    pallas_call x1, Pallas kernels: 32.5 us -> 28.8 us  [per_device(): pl.pallas_call(functools.partial(kernel, count_x), out_shape=[volume] * 3...]
where the time goes in v3:
time: 32.4 us; the launch traced here: 32.2 us
  Pallas kernels  28.8 us (89%)
  other arithmetic  2.21 us (7%)
  between operations  0.65 us (2%)
  local copies, waits for them, and re-layouts  0.62 us (2%)
    pallas_call x1, Pallas kernels, per_device(): pl.pallas_call(functools.partial(kernel, count_x), out_shape=[volume] * 3...  28.8 us
    add x1, other arithmetic, per_device(): return (wet * tracer, east + wet * grad_e, north + wet * grad_n, solved)  2.21 us

profile of v3, /device:TPU:0, one launch (start us, length us, event | category | flops | bytes accessed | tf_op | source)
XLA Modules:
  0.0 32.2 jit_solution(13298480548933008620)
XLA Ops:
  0.6 28.8 %shard_map.147 = (f32[10,32,256]{2,1,0:T(8,128)}, f32[10,32,256]{2,1,0:T(8,128)}, f32[10,32,256]{2,1,0:T(8,128)}, f32[32,256]{1,0:T(8,128)}, f32[32,256]{1,0:T(8...) custom-call(f32[10,32,256]{2,1,0:T(8,128)} %tracer_hbm.1, f32[10,32,256]{2,1,0:T(8,128)} %east_hbm.1, ...), custom_call_target="tpu_custom_call" | custom-call | tf_op jit(solution)/shard_map/pallas_call | solution.py:405
  29.4 0.0 copy-start
  29.4 2.2 %select_add_fusion = (f32[10,32,256]{2,1,0:T(8,128)}, f32[10,32,256]{2,1,0:T(8,128)}, f32[10,32,256]{2,1,0:T(8,128)}) fusion(f32[10,32,256]{2,1,0:T(8,128)} %get-tuple-element.15, f32[32,256]{1,0:T(8,128)} %get-tuple-element.16, f32[32,256]{1,0:T(8,128)} %get-tuple-element.11, f32[10,32,256]{2,1,0:T(8,128)} %get-tuple-element.13, ...), kind=kLoop, calls=%fused_computation | loop fusion | flops 491520 | bytes 2064384 | tf_op jit(solution)/shard_map/add | solution.py:416
  31.6 0.0 copy-done
  31.6 0.6 %copy.17 = f32[32,256]{1,0:T(8,128)} copy(f32[32,256]{1,0:T(8,128)S(1)} %copy-done) | data formatting | bytes 65536
Async XLA Ops:
  29.4 2.2 %copy-start = (f32[32,256]{1,0:T(8,128)S(1)}, f32[32,256]{1,0:T(8,128)}, u32[]{:S(2)}) copy-start(f32[32,256]{1,0:T(8,128)} %get-tuple-element.28) | copy-start | bytes 98308

commit v4 on v3

--- a/solution.py
+++ b/solution.py
@@ -17,7 +17,7 @@
     count_x,
     tracer_hbm, east_hbm, north_hbm, flow_e_hbm, flow_n_hbm, mixing_hbm, buoyancy_hbm, coriolis_hbm,
     depth_hbm, adj_surface_hbm, surface_diag_hbm, prior_hbm,
-    tracer_out, east_out, north_out, solution_out, grad_e_out, grad_n_out, depth_out,
+    tracer_out, east_out, north_out, planes_out,
     tracer_in, east_in, north_in, flow_e, flow_n, mixing, buoyancy, coriolis,
     depth_in, adj_surface, surface_diag, prior,
     rows_send, rows_recv,
@@ -25,7 +25,7 @@
     side_recv,
     plane_rows_send, plane_rows_recv, plane_corner_recv, plane_side_send, plane_side_recv,
     sum_rows_send, sum_rows_recv, sum_corner_recv, sum_side_send, sum_side_recv,
-    columns, moments, load_sem,
+    columns, moments, moved, load_sem, store_sem,
     rows_ss, rows_rs, corner_ss, corner_rs, side_ss, side_rs,
     plane_ss, plane_rs, sum_ss, sum_rs, moment_ss, moment_rs,
 ):
@@ -172,6 +172,10 @@
     def _(k):
         for copy in rows_copies(k):
             copy.start()
+
+    def store_copies(k):
+        return [pltpu.make_async_copy(moved.at[i, k], out.at[k], store_sem.at[i, k])
+                for i, out in enumerate((tracer_out, east_out, north_out))]
 
     columns[...] = jnp.zeros_like(columns)
     for copy in planes_copies() + corner_copies() + side_copies():
@@ -263,9 +267,10 @@
                      + take_n * to_north(n) + take_s * n_s + turn * e)
             t, e, n = t_new, e_new, n_new
         own = (slice(0, cols), slice(0, lanes))
-        tracer_out[k] = t[own]
-        east_out[k] = e[own]
-        north_out[k] = n[own]
+        for i, q in enumerate((t, e, n)):
+            moved[i, k] = q[own]
+        for copy in store_copies(k):
+            copy.start()
         columns[0] = columns[0] + e[own]
         columns[1] = columns[1] + n[own]
 
@@ -359,10 +364,15 @@
             rr = new
     gain = [g[:, 0:1] for g in gain]
     solved = start + gain[0] * v0 + gain[1] * v1 + gain[2] * v2
-    solution_out[...] = solved[0:cols, 0:lanes]
-    grad_e_out[...] = (0.5 * (to_east(solved) - to_west(solved)))[0:cols, 0:lanes]
-    grad_n_out[...] = (0.5 * (to_north(solved) - to_south(solved)))[0:cols, 0:lanes]
-    depth_out[...] = depth_own
+    planes_out[0] = (0.5 * (to_east(solved) - to_west(solved)))[0:cols, 0:lanes]
+    planes_out[1] = (0.5 * (to_north(solved) - to_south(solved)))[0:cols, 0:lanes]
+    planes_out[2] = depth_own
+    planes_out[3] = solved[0:cols, 0:lanes]
+
+    @pl.loop(0, levels)
+    def _(k):
+        for copy in store_copies(k):
+            copy.wait()
 
     for copy in planes_copies() + corner_copies() + side_copies() + sums_copies():
         copy.wait_send()
@@ -375,6 +385,38 @@
     @pl.loop(1, peers)
     def _(step):
         moment_copy(step).wait_send()
+
+
+def finish(
+    tracer_in, east_in, north_in, planes_in, tracer_out, east_out, north_out, solution_out,
+    tracer, east, north, planes, load_sem, store_sem,
+):
+    levels = tracer_in.shape[0]
+    parts = [pl.ds(0, levels // 2), pl.ds(levels // 2, levels - levels // 2)]
+    pairs = [(east_in, east, east_out), (north_in, north, north_out)]
+    first = pltpu.make_async_copy(planes_in, planes, load_sem.at[0])
+    last = pltpu.make_async_copy(tracer_in, tracer, load_sem.at[1])
+    loads = [pltpu.make_async_copy(src.at[part], held.at[part], load_sem.at[2 + 2 * i + j])
+             for i, part in enumerate(parts) for j, (src, held, _) in enumerate(pairs)]
+    stores = [pltpu.make_async_copy(held.at[part], dst.at[part], store_sem.at[2 + 2 * i + j])
+              for i, part in enumerate(parts) for j, (_, held, dst) in enumerate(pairs)]
+    whole = [pltpu.make_async_copy(planes.at[3], solution_out, store_sem.at[0]),
+             pltpu.make_async_copy(tracer, tracer_out, store_sem.at[1])]
+    for copy in [first] + loads + [last]:
+        copy.start()
+    first.wait()
+    whole[0].start()
+    depth = planes[2]
+    for i, part in enumerate(parts):
+        for j, (_, held, _) in enumerate(pairs):
+            loads[2 * i + j].wait()
+            for k in range(part.start, part.start + part.size):
+                held[k] = held[k] + jnp.where(depth > float(k), planes[j], 0.0)
+            stores[2 * i + j].start()
+    last.wait()
+    whole[1].start()
+    for copy in whole + stores:
+        copy.wait()
 
 
 def per_device(count_x, *args):
@@ -396,24 +438,33 @@
         pltpu.VMEM((5, cols, 128), f32), pltpu.VMEM((5, cols, 128), f32),
         pltpu.VMEM((2, 8, lanes), f32), pltpu.VMEM((2, 8, lanes), f32), pltpu.VMEM((2, 8, 128), f32),
         pltpu.VMEM((2, cols, 128), f32), pltpu.VMEM((2, cols, 128), f32),
-        pltpu.VMEM((2, cols, lanes), f32), pltpu.VMEM((peers, 8, 128), f32), dma((12,)),
+        pltpu.VMEM((2, cols, lanes), f32), pltpu.VMEM((peers, 8, 128), f32),
+        pltpu.VMEM((3, levels, cols, lanes), f32), dma((12,)), dma((3, levels)),
         dma((2, levels)), dma((2, levels)), dma((2,)), dma((2,)), dma((6,)), dma((6,)),
         dma((5,)), dma((5,)), dma((5,)), dma((5,)), dma((peers,)), dma((peers,)),
     ]
     volume = jax.ShapeDtypeStruct((levels, cols, lanes), f32)
     plane = jax.ShapeDtypeStruct((cols, lanes), f32)
-    tracer, east, north, solved, grad_e, grad_n, depth = pl.pallas_call(
+    tracer, east, north, planes = pl.pallas_call(
         functools.partial(kernel, count_x),
-        out_shape=[volume] * 3 + [plane] * 4,
+        out_shape=[volume] * 3 + [jax.ShapeDtypeStruct((4, cols, lanes), f32)],
         in_specs=[hbm] * 12,
-        out_specs=[vmem] * 7,
+        out_specs=[hbm] * 3 + [vmem],
         scratch_shapes=scratch,
         compiler_params=pltpu.CompilerParams(
             collective_id=0, has_side_effects=True, vmem_limit_bytes=60 * 1024 * 1024
         ),
     )(*args)
-    wet = (jnp.arange(levels, dtype=f32)[:, None, None] < depth[None]).astype(f32)
-    return wet * tracer, east + wet * grad_e, north + wet * grad_n, solved
+    return pl.pallas_call(
+        finish,
+        out_shape=[volume] * 3 + [plane],
+        in_specs=[hbm] * 4,
+        out_specs=[hbm] * 4,
+        scratch_shapes=[pltpu.VMEM((levels, cols, lanes), f32)] * 3 + [
+            pltpu.VMEM((4, cols, lanes), f32), dma((6,)), dma((6,)),
+        ],
+        compiler_params=pltpu.CompilerParams(vmem_limit_bytes=60 * 1024 * 1024),
+    )(tracer, east, north, planes)
 
 
 def solution(mesh):

time: 32.4 us -> 31.7 us (0.978)
  other arithmetic: 2.21 us -> 0 us
  Pallas kernels: 28.8 us -> 30.9 us
  local copies, waits for them, and re-layouts: 0.62 us -> 0 us
    add x1 -> x0, other arithmetic: 2.21 us -> none  [per_device(): return (wet * tracer, east + wet * grad_e, north + wet * grad_n, solved)]
    pallas_call x0 -> x1, Pallas kernels: none -> 2.16 us  [per_device(): pl.pallas_call(finish, out_shape=[volume] * 3 + [plane], in_specs=[hbm] *...]
    unnamed x3 -> x0, local copies, waits for them, and re-layouts: 0.62 us -> none
where the time goes in v4:
time: 31.7 us; the launch traced here: 31.6 us
  Pallas kernels  30.9 us (97%)
  between operations  0.64 us (2%)
    pallas_call x1, Pallas kernels, per_device(): pl.pallas_call(functools.partial(kernel, count_x), out_shape=[volume] * 3...  28.8 us
    pallas_call x1, Pallas kernels, per_device(): pl.pallas_call(finish, out_shape=[volume] * 3 + [plane], in_specs=[hbm] *...  2.16 us

profile of v4, /device:TPU:0, one launch (start us, length us, event | category | flops | bytes accessed | tf_op | source)
XLA Modules:
  0.0 31.6 jit_solution(233753352199231370)
XLA Ops:
  0.6 28.8 %shard_map.147 = (f32[10,32,256]{2,1,0:T(8,128)}, f32[10,32,256]{2,1,0:T(8,128)}, f32[10,32,256]{2,1,0:T(8,128)}, f32[4,32,256]{2,1,0:T(8,128)}) custom-call(f32[10,32,256]{2,1,0:T(8,128)} %tracer_hbm.1, f32[10,32,256]{2,1,0:T(8,128)} %east_hbm.1, f32[10,32,256]{2,1,0:T(8,128)} %north_hbm.1, f32[10,32,256]{2,1,0:T(8,128)} %flow_e_hbm.1, ...), custom_call_target="tpu_custom_call" | custom-call | tf_op jit(solution)/shard_map/pallas_call | solution.py:448
  29.4 2.2 %shard_map.148 = (f32[10,32,256]{2,1,0:T(8,128)}, f32[10,32,256]{2,1,0:T(8,128)}, f32[10,32,256]{2,1,0:T(8,128)}, f32[32,256]{1,0:T(8,128)}) custom-call(f32[10,32,256]{2,1,0:T(8,128)} %get-tuple-element.8.tracer_in, f32[10,32,256]{2,1,0:T(8,128)} %get-tuple-element.9.east_in, f32[10,32,256]{2,1,0:T(8,128)} %get-tuple-element.10.north_in, ...), custom_call_target="tpu_custom_call" | custom-call | tf_op jit(solution)/shard_map/pallas_call | solution.py:458

commit v5 on v4

--- a/solution.py
+++ b/solution.py
@@ -331,6 +331,19 @@
     def _(step):
         moment_copy(step).start()
 
+    @pl.loop(0, levels)
+    def _(k):
+        for copy in store_copies(k):
+            copy.wait()
+
+    for copy in planes_copies() + corner_copies() + side_copies() + sums_copies():
+        copy.wait_send()
+
+    @pl.loop(levels - window, levels)
+    def _(k):
+        for copy in rows_copies(k):
+            copy.wait_send()
+
     @pl.loop(1, peers)
     def _(step):
         source = lax.rem(me + step, peers)
@@ -368,19 +381,6 @@
     planes_out[1] = (0.5 * (to_north(solved) - to_south(solved)))[0:cols, 0:lanes]
     planes_out[2] = depth_own
     planes_out[3] = solved[0:cols, 0:lanes]
-
-    @pl.loop(0, levels)
-    def _(k):
-        for copy in store_copies(k):
-            copy.wait()
-
-    for copy in planes_copies() + corner_copies() + side_copies() + sums_copies():
-        copy.wait_send()
-
-    @pl.loop(levels - window, levels)
-    def _(k):
-        for copy in rows_copies(k):
-            copy.wait_send()
 
     @pl.loop(1, peers)
     def _(step):

time: 31.7 us -> 31.6 us (level)
  no operation moved by 1% of the time
where the time goes in v5:
time: 31.6 us; the launch traced here: 31.4 us
  Pallas kernels  30.8 us (97%)
  between operations  0.64 us (2%)
    pallas_call x1, Pallas kernels, per_device(): pl.pallas_call(functools.partial(kernel, count_x), out_shape=[volume] * 3...  28.6 us
    pallas_call x1, Pallas kernels, per_device(): pl.pallas_call(finish, out_shape=[volume] * 3 + [plane], in_specs=[hbm] *...  2.16 us

profile of v5, /device:TPU:0, one launch (start us, length us, event | category | flops | bytes accessed | tf_op | source)
XLA Modules:
  0.0 31.4 jit_solution(2417271021088981567)
XLA Ops:
  0.6 28.6 %shard_map.147 = (f32[10,32,256]{2,1,0:T(8,128)}, f32[10,32,256]{2,1,0:T(8,128)}, f32[10,32,256]{2,1,0:T(8,128)}, f32[4,32,256]{2,1,0:T(8,128)}) custom-call(f32[10,32,256]{2,1,0:T(8,128)} %tracer_hbm.1, f32[10,32,256]{2,1,0:T(8,128)} %east_hbm.1, f32[10,32,256]{2,1,0:T(8,128)} %north_hbm.1, f32[10,32,256]{2,1,0:T(8,128)} %flow_e_hbm.1, ...), custom_call_target="tpu_custom_call" | custom-call | tf_op jit(solution)/shard_map/pallas_call | solution.py:448
  29.3 2.2 %shard_map.148 = (f32[10,32,256]{2,1,0:T(8,128)}, f32[10,32,256]{2,1,0:T(8,128)}, f32[10,32,256]{2,1,0:T(8,128)}, f32[32,256]{1,0:T(8,128)}) custom-call(f32[10,32,256]{2,1,0:T(8,128)} %get-tuple-element.8.tracer_in, f32[10,32,256]{2,1,0:T(8,128)} %get-tuple-element.9.east_in, f32[10,32,256]{2,1,0:T(8,128)} %get-tuple-element.10.north_in, ...), custom_call_target="tpu_custom_call" | custom-call | tf_op jit(solution)/shard_map/pallas_call | solution.py:458
